TPU v7x, 32 devices: a whole 2x2x4 slice. The times are simulated.
32 devices in a mesh: tm: 8 (over z, y), freq: 4 (over x, core).
Axes of the slice: x: 2, y: 2, z: 4, core: 2. Of those that a mesh axis runs over, the one named last changes fastest.
Arguments:
- visibility: float32 [64, 2, 4096, 1024], P('freq', None, 'tm'), may hold values from -6 to 6
- codebook: bfloat16 [16, 8, 64, 128], replicated, may hold values from -0.1875 to 0.1875
- block_index: int32 [8, 64, 16, 16], P('tm', 'freq'), may hold values from -1 to 7, as said below
- block_scale: float32 [8, 64, 16, 16], P('tm', 'freq'), may hold values from 0.5 to 2
- fg_basis: float32 [16, 64, 64], replicated, may hold values from -0.75 to 0.75
- fg_count: int32 [8], P('tm'), may hold values from 1 to 32
Outputs:
- filtered: float32 [8, 64, 16, 128], P('tm', 'freq')
Inputs may be any that keep to these rules, and one draw needn't show every extreme that they name: `block_index`: -1 marks an absent block; block (k, f, j, l) is absent whenever 64 * l + 63 < 127 * k; other entries name a pattern.
All inputs are finite; a program needn't handle non-finite values.
Results may differ from a plain program's by a relative error of at most 0.014.
Values may be sent and summed in bfloat16 or wider, within the bound.
A program may use at most 128 MiB of HBM per device.

v0:
```python
import math

import jax
import jax.numpy as jnp
from jax import lax
from jax.sharding import PartitionSpec as P

ELLS = 1024


def realify(codebook):
    half = codebook.shape[-1] // 2
    real_part = codebook[..., :half]
    imag_part = codebook[..., half:]
    upper = jnp.concatenate([real_part, -imag_part], axis=-1)
    lower = jnp.concatenate([imag_part, real_part], axis=-1)
    return jnp.concatenate([upper, lower], axis=-2)


def phases(mode_values, time_index, sidereal_period):
    product = mode_values[:, None] * time_index[None, :] % sidereal_period
    angle = product.astype(jnp.float32) * jnp.float32(2.0 * math.pi / sidereal_period)
    return (jnp.cos(angle), jnp.sin(angle))


def apply_dft(cosine_table, sine_table, samples, norm_factor):
    with_cos = jnp.einsum("mt,fctb->mfcb", cosine_table, samples, precision=lax.Precision.HIGHEST)
    with_sin = jnp.einsum("mt,fctb->mfcb", sine_table, samples, precision=lax.Precision.HIGHEST)
    real_part = with_cos[:, :, 0] + with_sin[:, :, 1]
    imag_part = with_cos[:, :, 1] - with_sin[:, :, 0]
    return jnp.stack([real_part, imag_part], axis=2) * norm_factor


def local(visibility, codebook, block_index, block_scale, fg_basis, fg_count):
    tm_count = lax.axis_size("tm")
    chans_dev = visibility.shape[0]
    time_dev = visibility.shape[2]
    base_all = visibility.shape[3]
    modes_dev = block_index.shape[0]
    modes_all = modes_dev * tm_count
    mode_step = 2 * (ELLS // (2 * modes_all)) - 1
    code_count = codebook.shape[1]
    block_len = codebook.shape[2]
    bblocks = base_all // block_len
    sidereal_period = time_dev * tm_count
    norm_factor = float(sidereal_period) ** (-0.5)
    tm_pos = lax.axis_index("tm")
    time_index = tm_pos * time_dev + jnp.arange(time_dev, dtype=jnp.int32)
    mode_values = mode_step * jnp.arange(modes_dev * lax.axis_size("tm"), dtype=jnp.int32)
    cosine_table, sine_table = phases(mode_values, time_index, sidereal_period)
    spectra = lax.psum_scatter(
        apply_dft(cosine_table, sine_table, visibility, norm_factor),
        "tm",
        scatter_dimension=0,
        tiled=True,
    ).astype(jnp.bfloat16)
    vectors = spectra.reshape(modes_dev, chans_dev, 2, bblocks, block_len)
    vectors = jnp.transpose(vectors, (0, 1, 3, 2, 4)).reshape(
        modes_dev, chans_dev, bblocks, 2 * block_len
    )
    vectors = vectors.astype(jnp.float32)
    code_matrix = realify(codebook).astype(jnp.float32)
    block_selector = jnp.where(
        block_index[..., None] == jnp.arange(code_count, dtype=jnp.int32),
        block_scale[..., None],
        jnp.float32(0.0),
    )
    combined = jnp.einsum(
        "mfblp,mfbi->mflpi", block_selector, vectors, precision=lax.Precision.HIGHEST
    )
    weights = jnp.einsum("mflpi,lpij->mflj", combined, code_matrix, precision=lax.Precision.HIGHEST)
    weights_bf = weights.astype(jnp.bfloat16)
    fr_pos = lax.axis_index("freq")
    weights_full = lax.optimization_barrier(weights_bf).astype(jnp.float32)
    basis_rows = lax.dynamic_slice_in_dim(fg_basis, fr_pos * chans_dev, chans_dev, 1)
    summed = lax.psum_scatter(
        jnp.einsum(
            "lfk,mflj->kmlj", basis_rows, weights_full, precision=lax.Precision.HIGHEST
        ).astype(jnp.bfloat16),
        "freq",
        scatter_dimension=0,
        tiled=True,
    ).astype(jnp.float32)
    filtered = jnp.transpose(summed, (1, 0, 2, 3))
    mode_index = fr_pos * chans_dev + jnp.arange(chans_dev, dtype=jnp.int32)
    retained = mode_index[None, :] >= fg_count[:, None]
    return jnp.where(retained[:, :, None, None], filtered, jnp.float32(0.0))


def solution(mesh):
    placed = (
        P("freq", None, "tm", None),
        P(),
        P("tm", "freq", None, None),
        P("tm", "freq", None, None),
        P(),
        P("tm"),
    )
    return jax.shard_map(
        local, mesh=mesh, in_specs=placed, out_specs=P("tm", "freq", None, None), check_vma=False
    )
```

profile of v0, /device:TPU:0, one launch (start us, length us, event | category | flops | bytes accessed | tf_op | source)
XLA Modules:
  0.0 189.6 jit_solution(829897856753262792)
XLA Ops:
  6.5 0.0 copy-start
  6.5 0.0 reduce-scatter.3.cloned.1.call-start
  6.5 36.7 %fusion.30 = f32[8,16,2,1024]{3,0,2,1:T(8,128)S(1)} fusion(f32[16,2,512,1024]{3,2,1,0:T(8,128)} %param.6, s32[512]{0:T(512)S(1)} %iota_add_fusion, s32[8]{0:T(128)S(1)} %iota_multiply_fusion), kind=kOutput, calls=%fused_computation.35 | convolution fusion | flops 1610670080 | bytes 68159520 | tf_op jit(solution)/shard_map/mt,fctb->mfcb/dot_general | solution.py:28
  43.2 39.0 %fusion.32 = f32[8,16,2,1024]{3,0,2,1:T(8,128)} fusion(f32[16,2,512,1024]{3,2,1,0:T(8,128)} %param.6, s32[512]{0:T(512)S(1)} %iota_add_fusion, s32[8]{0:T(128)S(1)} %iota_multiply_fusion), kind=kOutput, calls=%fused_computation.37 | convolution fusion | flops 1610670080 | bytes 68159520 | tf_op jit(solution)/shard_map/mt,fctb->mfcb/dot_general | solution.py:27
  82.2 0.0 copy-start.2
  82.2 0.0 copy-start.3
  82.2 0.0 copy-start.1
  82.2 1.5 slice_add_fusion
  83.7 0.1 maximum_multiply_fusion
  83.8 1.6 copy.13
  85.5 0.0 reduce-scatter.3.cloned.1.call-update
  85.5 0.0 reduce-scatter.5.cloned.1.call-start
  85.5 0.0 copy-done.2
  85.5 0.1 copy.11
  85.6 0.0 copy-done.3
  85.7 0.1 copy.12
  85.8 0.0 copy-done.1
  85.8 3.5 %slice_negate_fusion = (bf16[16,8,64,64]{3,2,1,0:T(8,128)(2,1)}, bf16[16,8,64,64]{3,2,1,0:T(8,128)(2,1)}, bf16[16,8,64,64]{3,2,1,0:T(8,128)(2,1)}) fusion(bf16[16,8,64,128]{3,2,1,0:T(8,128)(2,1)S(1)} %copy-done.1), kind=kLoop, calls=%fused_computation.55 | loop fusion | flops 524288 | bytes 5242880 | tf_op jit(solution)/shard_map/neg | solution.py:15
  89.3 62.6 %reduce-scatter.3.cloned.1.call-done = f32[1,16,2,1024]{3,1,2,0:T(8,128)} async-done(((f32[8,16,2,1024]{3,1,2,0:T(8,128)}), f32[1,16,2,1024]{3,1,2,0:T(8,128)}) %reduce-scatter.3.cloned.1.call-update) | async-done | bytes 131088 | tf_op jit(solution)/shard_map/reduce_scatter | solution.py:51
  151.9 0.9 convert_element_type.29
  152.8 0.1 reshape.61
  152.9 0.1 copy.14
  153.1 0.1 reshape.67
  153.2 0.7 fusion.19
  153.9 6.7 %fusion.15 = bf16[1,16,16,128]{3,1,2,0:T(8,128)(2,1)S(1)} fusion(bf16[16,8,64,64]{3,2,1,0:T(8,128)(2,1)} %get-tuple-element.9, bf16[16,8,64,64]{3,2,1,0:T(8,128)(2,1)} %get-tuple-element.8, bf16[16,8,64,64]{3,2,1,0:T(8,128)(2,1)} %get-tuple-element.7, f32[16,16,8,128]{3,2,1,0:T(8,128)S(1)} %fusion.19), kind=kOutput, calls=%fused_computation.12 | convolution fusion | flops 419463168 | bytes 4259840 | tf_op jit(solution)/shard_map/mflpi,lpij->mflj/dot_general | solution.py:71
  160.6 0.0 copy-done
  160.6 1.3 fusion.8
  161.9 0.0 reduce-scatter.5.cloned.1.call-update
  162.6 18.6 %reduce-scatter.5.cloned.1.call-done = bf16[16,1,16,128]{3,0,2,1:T(8,128)(2,1)} async-done(((bf16[64,1,16,128]{3,0,2,1:T(8,128)(2,1)}), bf16[16,1,16,128]{3,0,2,1:T(8,128)(2,1)}) %reduce-scatter.5.cloned.1.call-update) | async-done | bytes 65552 | tf_op jit(solution)/shard_map/reduce_scatter | solution.py:76
  181.2 0.9 convert_select_fusion
  182.1 0.7 copy.16
  (3 shorter events, 0.0 us)
Async XLA Ops:
  6.5 154.1 %copy-start = (f32[16,64,64]{2,1,0:T(8,128)S(1)}, f32[16,64,64]{2,1,0:T(8,128)}, u32[]{:S(2)}) copy-start(f32[16,64,64]{2,1,0:T(8,128)} %param.10) | copy-start | bytes 786436
  6.5 145.3 %reduce-scatter.3.cloned.1.call-start = ((), (), s32[]{:S(2)}) async-start(), calls=%async_computation.2 | async-start | bytes 1179648 | tf_op jit(solution)/shard_map/reduce_scatter | solution.py:51
  82.2 3.3 %copy-start.2 = (s32[1,16,16,16]{3,2,1,0:T(8,128)S(1)}, s32[1,16,16,16]{3,2,1,0:T(8,128)}, u32[]{:S(2)}) copy-start(s32[1,16,16,16]{3,2,1,0:T(8,128)} %param.8) | copy-start | bytes 49156
  82.2 3.4 %copy-start.3 = (f32[1,16,16,16]{3,2,1,0:T(8,128)S(1)}, f32[1,16,16,16]{3,2,1,0:T(8,128)}, u32[]{:S(2)}) copy-start(f32[1,16,16,16]{3,2,1,0:T(8,128)} %param.9) | copy-start | bytes 49156
  82.2 3.5 %copy-start.1 = (bf16[16,8,64,128]{3,2,1,0:T(8,128)(2,1)S(1)}, bf16[16,8,64,128]{3,2,1,0:T(8,128)(2,1)}, u32[]{:S(2)}) copy-start(bf16[16,8,64,128]{3,2,1,0:T(8,128)(2,1)} %param.7) | copy-start | bytes 6291460
  85.5 95.7 %reduce-scatter.5.cloned.1.call-start = ((), (), s32[]{:S(2)}) async-start(), calls=%async_computation.3 | async-start | bytes 327680 | tf_op jit(solution)/shard_map/reduce_scatter | solution.py:76
Sparse Core Ops, SparseCore 0:
  85.6 66.2 reduce-scatter.2
  162.1 19.0 reduce-scatter.4
where the time goes:
time: 190 us
  matrix products  84.4 us (44%)
  waiting for transfers between devices  81.2 us (43%)
  between operations  14.2 us (7%)
  other arithmetic  6.97 us (4%)
  local copies, waits for them, and re-layouts  2.89 us (2%)
    reduce_scatter x1, waiting for transfers between devices, local(): lax.psum_scatter(apply_dft(cosine_table, sine_table, visibility, norm_fac...  62.6 us
    dot_general x1, matrix products, apply_dft(): jnp.einsum('mt,fctb->mfcb', cosine_table, samples, precision=lax.Precisio...  39 us
    dot_general x1, matrix products, apply_dft(): jnp.einsum('mt,fctb->mfcb', sine_table, samples, precision=lax.Precision....  36.7 us
    reduce_scatter x1, waiting for transfers between devices, local(): lax.psum_scatter(jnp.einsum('lfk,mflj->kmlj', basis_rows, weights_full, p...  18.6 us
    dot_general x1, matrix products, local(): jnp.einsum('mflpi,lpij->mflj', combined, code_matrix, precision=lax.Preci...  6.74 us
  transfers between devices with their start and end apart: 2, of which 2 were waited for; matrix products, arithmetic and copies ran while one was open for 2% of the time, Pallas kernels for 0%

commit v1 on v0

v1 whole, which is shorter than its diff:
```python
import functools
import math

import jax
import jax.numpy as jnp
import numpy as np
from jax import lax
from jax.experimental import pallas as pl
from jax.experimental.pallas import tpu as pltpu
from jax.sharding import PartitionSpec as P

ELLS = 1024
LANES = 256
SUB = 8
MESH = pl.DeviceIdType.MESH
NT = (((1,), (1,)), ((), ()))


def phase_tables(parts, time_dev, modes_all):
    period = parts * time_dev
    step = 2 * (ELLS // (2 * modes_all)) - 1
    modes = step * np.arange(modes_all, dtype=np.int64)
    times = np.arange(period, dtype=np.int64)
    angle = (modes[:, None] * times[None, :] % period) * (2.0 * math.pi / period)
    cosine = np.cos(angle).reshape(modes_all, parts, time_dev).transpose(1, 0, 2)
    sine = np.sin(angle).reshape(modes_all, parts, time_dev).transpose(1, 0, 2)
    real_rows = np.concatenate([cosine, sine], axis=2)
    imag_rows = np.concatenate([-sine, cosine], axis=2)
    return np.concatenate([real_rows, imag_rows], axis=1).astype(jnp.bfloat16)


def kernel(
    n_tm, n_fr, norm,
    tab_hbm, vis, cb_hbm, idx_hbm, scl_hbm, bas_hbm, count,
    out,
    tab, cb, idx, scl, bas, vbuf, acc, send, recv, idx_t, scl_t, sel, vec, comb, filt, gath,
    small_sem, vis_sem, send_sem, recv_sem, gsend_sem, grecv_sem,
):
    tm = lax.axis_index("tm")
    fr = lax.axis_index("freq")
    modes = tab.shape[0] // 2
    samples = vbuf.shape[2]
    chans = vis.shape[0]
    halves = chans // SUB
    lane_groups = vis.shape[3] // LANES
    groups = lane_groups * halves
    blocks = vec.shape[1]
    bands, codes = cb.shape[0], cb.shape[1]
    f32, bf16 = jnp.float32, jnp.bfloat16

    smalls = [
        pltpu.make_async_copy(src, dst, small_sem.at[i])
        for i, (src, dst) in enumerate(
            ((idx_hbm, idx), (scl_hbm, scl), (tab_hbm.at[tm], tab), (bas_hbm, bas), (cb_hbm, cb))
        )
    ]

    def fetch(g, slot):
        lanes = pl.ds(pl.multiple_of((g // halves) * LANES, LANES), LANES)
        chan = (g % halves) * SUB + slot
        return pltpu.make_async_copy(
            vis.at[chan, :, :, lanes], vbuf.at[slot], vis_sem.at[slot]
        )

    for copy in smalls[:3]:
        copy.start()
    for slot in range(SUB):
        fetch(0, slot).start()
    for copy in smalls[3:]:
        copy.start()

    barrier = pltpu.get_barrier_semaphore()

    @pl.loop(1, n_tm)
    def _(d):
        peer = lax.rem(tm + d, n_tm)
        pl.semaphore_signal(barrier, inc=1, device_id={"tm": peer}, device_id_type=MESH)

    for d in range(1, n_fr):
        peer = lax.rem(fr + d, n_fr)
        pl.semaphore_signal(barrier, inc=1, device_id={"freq": peer}, device_id_type=MESH)

    smalls[0].wait()
    smalls[1].wait()
    wide = blocks * chans
    eye = (
        lax.broadcasted_iota(jnp.int32, (bands, bands), 0)
        == lax.broadcasted_iota(jnp.int32, (bands, bands), 1)
    ).astype(f32).astype(bf16)
    for src, dst in ((idx, idx_t), (scl, scl_t)):
        rows = jnp.concatenate([src[:, j, :] for j in range(blocks)], axis=0)
        rows = rows.astype(f32).astype(bf16)
        dst[...] = lax.dot_general(eye, rows, NT, preferred_element_type=f32)
    same_chan = (
        lax.broadcasted_iota(jnp.int32, (chans, wide), 1) % chans
        == lax.broadcasted_iota(jnp.int32, (chans, wide), 0)
    )

    @pl.loop(0, bands)
    def _(l):
        which = jnp.broadcast_to(idx_t[pl.ds(l, 1), :], (chans, wide))
        which = jnp.where(same_chan, which, f32(-1.0))
        scale = jnp.broadcast_to(scl_t[pl.ds(l, 1), :], (chans, wide))
        for p in range(codes):
            row, col = (p // 2) * chans, (p % 2) * wide
            sel[l, row : row + chans, col : col + wide] = jnp.where(
                which == f32(p), scale, f32(0.0)
            ).astype(bf16)

    smalls[2].wait()
    pl.semaphore_wait(barrier, n_tm - 1 + n_fr - 1)

    def take(lane_group):
        parts = []
        for half in range(halves):
            g = lane_group * halves + half
            pltpu.make_async_copy(recv.at[g], recv.at[g], recv_sem.at[g]).wait()
            parts.append(jnp.sum(recv[g].astype(f32), axis=0))
        real = jnp.concatenate([part[:SUB] for part in parts], axis=0)
        imag = jnp.concatenate([part[SUB:] for part in parts], axis=0)
        left = lax.broadcasted_iota(jnp.int32, (chans, 128), 1) < 64
        zero = jnp.zeros((chans, 128), f32)
        for pair in range(LANES // 128):
            r = real[:, pair * 128 : pair * 128 + 128]
            i = imag[:, pair * 128 : pair * 128 + 128]
            rr, ri = pltpu.roll(r, 64, 1), pltpu.roll(i, 64, 1)
            even = lane_group * (LANES // 64) + 2 * pair

            def put(first, j, a, b):
                if first:
                    a, b = jnp.where(left, a, zero), jnp.where(left, b, zero)
                else:
                    a, b = jnp.where(left, zero, a), jnp.where(left, zero, b)
                vec[0 if first else 1, j] = jnp.concatenate([a, b], axis=1).astype(bf16)

            put(True, even, r, i)
            put(False, even, rr, ri)
            put(True, even + 1, rr, ri)
            put(False, even + 1, r, i)

    @pl.loop(0, lane_groups)
    def _(lane_group):
        @pl.loop(0, halves)
        def _(half):
            g = lane_group * halves + half
            for slot in range(SUB):
                fetch(g, slot).wait()
                block = vbuf[slot].reshape(2 * samples, LANES).astype(bf16)
                sums = jnp.dot(tab[...], block, preferred_element_type=f32)
                acc[:, slot, :] = sums[:modes]
                acc[:, SUB + slot, :] = sums[modes:]

                @pl.when(g + 1 < groups)
                def _():
                    fetch(g + 1, slot).start()

            send[g] = (acc[...] * f32(norm)).astype(bf16)
            pltpu.make_async_copy(send.at[g, tm], recv.at[g, tm], recv_sem.at[g]).start()

            @pl.loop(1, n_tm)
            def _(d):
                peer = lax.rem(tm + d, n_tm)
                pltpu.make_async_remote_copy(
                    src_ref=send.at[g, peer],
                    dst_ref=recv.at[g, tm],
                    send_sem=send_sem.at[g],
                    recv_sem=recv_sem.at[g],
                    device_id={"tm": peer},
                    device_id_type=MESH,
                ).start()

        @pl.when(lane_group > 0)
        def _():
            take(lane_group - 1)

    smalls[3].wait()
    smalls[4].wait()
    part = bands // 2
    all_chans = bas.shape[1]
    rows = chans * part
    pick = (
        lax.broadcasted_iota(jnp.int32, (rows, all_chans), 1)
        == lax.broadcasted_iota(jnp.int32, (rows, all_chans), 0) // part + fr * chans
    ).astype(f32).astype(bf16)
    basis = bas[...].reshape(bands * all_chans, all_chans).astype(bf16)
    spread = lax.dot_general(pick, basis, NT, preferred_element_type=f32)
    same_band = (
        lax.broadcasted_iota(jnp.int32, spread.shape, 1) // all_chans % part
        == lax.broadcasted_iota(jnp.int32, spread.shape, 0) % part
    )
    filt[...] = jnp.where(same_band, spread, f32(0.0)).astype(bf16)

    take(lane_groups - 1)

    vectors = vec[...].reshape(2 * wide, LANES)
    left = lax.broadcasted_iota(jnp.int32, (chans, 128), 1) < 64
    pairs = codes // 2

    def share(h, d):
        peer = lax.rem(fr + d, n_fr)
        mine = gath.at[fr, pl.ds(h * part, part)]
        return pltpu.make_async_remote_copy(
            src_ref=mine,
            dst_ref=mine,
            send_sem=gsend_sem.at[h, d - 1],
            recv_sem=grecv_sem.at[h, d - 1],
            device_id={"freq": peer},
            device_id_type=MESH,
        )

    for h in range(2):
        chosen = sel[h * part : (h + 1) * part].reshape(part * pairs * chans, 2 * wide)
        comb[...] = (
            jnp.dot(chosen, vectors, preferred_element_type=f32)
            .astype(bf16)
            .reshape(part, pairs * chans, LANES)
        )
        for k in range(part):
            c = comb[k]
            lhs = jnp.concatenate(
                [
                    jnp.concatenate(
                        [c[p * chans : (p + 1) * chans, o : o + 128] for p in range(pairs)], axis=1
                    )
                    for o in (0, 128)
                ],
                axis=0,
            )
            weights = cb[h * part + k].reshape(codes * 64, 128)
            both = jnp.dot(lhs, weights, preferred_element_type=f32)
            upper, lower = both[:chans], both[chans:]
            projected = jnp.where(left, upper, -upper) + pltpu.roll(lower, 64, 1)
            gath[fr, h * part + k] = projected.astype(bf16)
        for d in range(1, n_fr):
            share(h, d).start()

    kept = (
        lax.broadcasted_iota(jnp.int32, (chans, part, 128), 0) + fr * chans >= count[0]
    )
    for h in range(2):
        for d in range(1, n_fr):
            share(h, d).wait_recv()
        rows_in = jnp.concatenate(
            [gath[s, h * part + k] for k in range(part) for s in range(n_fr)], axis=0
        )
        depth = part * all_chans
        got = jnp.dot(
            filt[:, h * depth : (h + 1) * depth], rows_in, preferred_element_type=f32
        ).reshape(chans, part, 128)
        out[:, h * part : (h + 1) * part, :] = jnp.where(kept, got, f32(0.0))

    for h in range(2):
        for d in range(1, n_fr):
            share(h, d).wait_send()

    @pl.loop(0, groups)
    def _(g):
        sent = send.at[g, pl.ds(0, n_tm - 1)]
        pltpu.make_async_copy(sent, sent, send_sem.at[g]).wait()


def local(n_tm, n_fr, visibility, codebook, block_index, block_scale, fg_basis, fg_count):
    chans, _, time_dev, base_all = visibility.shape
    modes_all = block_index.shape[0] * n_tm
    bands, codes, block_len, width = codebook.shape
    blocks = base_all // block_len
    all_chans = fg_basis.shape[1]
    groups = base_all // LANES * (chans // SUB)
    wide = blocks * chans
    norm = float(time_dev * n_tm) ** -0.5
    tables = jnp.asarray(phase_tables(n_tm, time_dev, modes_all))
    anywhere = pl.BlockSpec(memory_space=pl.ANY)
    f32, bf16 = jnp.float32, jnp.bfloat16
    out = pl.pallas_call(
        functools.partial(kernel, n_tm, n_fr, norm),
        out_shape=jax.ShapeDtypeStruct((chans, bands, width), f32),
        in_specs=[anywhere] * 6 + [pl.BlockSpec(memory_space=pltpu.SMEM)],
        out_specs=pl.BlockSpec(memory_space=pltpu.VMEM),
        scratch_shapes=[
            pltpu.VMEM(tables.shape[1:], bf16),
            pltpu.VMEM(codebook.shape, bf16),
            pltpu.VMEM(block_index.shape[1:], jnp.int32),
            pltpu.VMEM(block_scale.shape[1:], f32),
            pltpu.VMEM(fg_basis.shape, f32),
            pltpu.VMEM((SUB, 2, time_dev, LANES), f32),
            pltpu.VMEM((modes_all, 2 * SUB, LANES), f32),
            pltpu.VMEM((groups, n_tm, 2 * SUB, LANES), bf16),
            pltpu.VMEM((groups, n_tm, 2 * SUB, LANES), bf16),
            pltpu.VMEM((bands, wide), f32),
            pltpu.VMEM((bands, wide), f32),
            pltpu.VMEM((bands, codes // 2 * chans, 2 * wide), bf16),
            pltpu.VMEM((2, blocks, chans, LANES), bf16),
            pltpu.VMEM((bands // 2, codes // 2 * chans, LANES), bf16),
            pltpu.VMEM((chans * (bands // 2), bands * all_chans), bf16),
            pltpu.VMEM((n_fr, bands, chans, width), bf16),
            pltpu.SemaphoreType.DMA((5,)),
            pltpu.SemaphoreType.DMA((SUB,)),
            pltpu.SemaphoreType.DMA((groups,)),
            pltpu.SemaphoreType.DMA((groups,)),
            pltpu.SemaphoreType.DMA((2, n_fr - 1)),
            pltpu.SemaphoreType.DMA((2, n_fr - 1)),
        ],
        compiler_params=pltpu.CompilerParams(
            collective_id=0, has_side_effects=True, vmem_limit_bytes=48 * 1024 * 1024
        ),
        name="mmode",
    )(
        tables,
        visibility,
        codebook,
        block_index.reshape(block_index.shape[1:]),
        block_scale.reshape(block_scale.shape[1:]),
        fg_basis,
        fg_count,
    )
    return out[None]


def solution(mesh):
    placed = (
        P("freq", None, "tm", None),
        P(),
        P("tm", "freq", None, None),
        P("tm", "freq", None, None),
        P(),
        P("tm"),
    )
    return jax.shard_map(
        functools.partial(local, mesh.shape["tm"], mesh.shape["freq"]),
        mesh=mesh,
        in_specs=placed,
        out_specs=P("tm", "freq", None, None),
        check_vma=False,
    )
```

time: 190 us -> 41.5 us (0.22)
  matrix products: 84.4 us -> 0 us
  waiting for transfers between devices: 81.2 us -> 0 us
  Pallas kernels: 0 us -> 34.6 us
  between operations: 14.2 us -> 0.67 us
  other arithmetic: 6.97 us -> 0 us
  local copies, waits for them, and re-layouts: 2.89 us -> 6.04 us
    dot_general x5 -> x0, matrix products: 84.4 us -> none  [the longest x1 39 us: apply_dft(): jnp.einsum('mt,fctb->mfcb', cosine_table, samples, precision=lax.Precisio...]
    reduce_scatter x2 -> x0, waiting for transfers between devices: 81.1 us -> none  [the longest x1 62.6 us: local(): lax.psum_scatter(apply_dft(cosine_table, sine_table, visibility, norm_fac...]
    pallas_call x0 -> x1, Pallas kernels: none -> 34.6 us  [local(): pl.pallas_call(functools.partial(kernel, n_tm, n_fr, norm), out_shape=jax...]
    unnamed x8 -> x11, local copies, waits for them, and re-layouts: 0.02 us -> 6.04 us
    neg x1 -> x0, other arithmetic: 3.52 us -> none  [realify(): upper = jnp.concatenate([real_part, -imag_part], axis=-1)]
  transfers between devices with their start and end apart: 2 -> 0, of which waited for: 2 -> 0; matrix products, arithmetic and copies ran while one was open for 2% -> 0% of each run, Pallas kernels for 0% -> 0%
where the time goes in v1:
time: 41.5 us; the launch traced here: 41.3 us
  Pallas kernels  34.6 us (83%)
  local copies, waits for them, and re-layouts  6.04 us (15%)
  between operations  0.67 us (2%)
    pallas_call x1, Pallas kernels, local(): pl.pallas_call(functools.partial(kernel, n_tm, n_fr, norm), out_shape=jax...  34.6 us
    unnamed x11, local copies, waits for them, and re-layouts  6.04 us

profile of v1, /device:TPU:0, one launch (start us, length us, event | category | flops | bytes accessed | tf_op | source)
XLA Modules:
  0.0 41.3 jit_solution(250693866616799792)
XLA Ops:
  0.7 0.0 copy-start
  0.7 1.6 %copy-done = bf16[16,8,64,128]{3,2,1,0:T(8,128)(2,1)S(1)} copy-done((bf16[16,8,64,128]{3,2,1,0:T(8,128)(2,1)S(1)}, bf16[16,8,64,128]{3,2,1,0:T(8,128)(2,1)}, u32[]{:S(2)}) %copy-start) | copy-done | bytes 2097176
  2.2 0.0 copy-start.1
  2.2 1.0 %copy-done.1 = f32[16,64,64]{2,1,0:T(8,128)S(1)} copy-done((f32[16,64,64]{2,1,0:T(8,128)S(1)}, f32[16,64,64]{2,1,0:T(8,128)}, u32[]{:S(2)}) %copy-start.1) | copy-done | bytes 262168
  3.3 0.0 copy-start.2
  3.3 0.9 %copy-done.2 = bf16[8,16,1024]{2,1,0:T(8,128)(2,1)S(1)} copy-done((bf16[8,16,1024]{2,1,0:T(8,128)(2,1)S(1)}, bf16[8,16,1024]{2,1,0:T(8,128)(2,1)}, u32[]{:S(2)}) %copy-start.2) | copy-done | bytes 262168
  4.2 0.0 copy-start.3
  4.2 0.9 %copy-done.3 = s32[1,16,16,16]{3,2,1,0:T(8,128)S(1)} copy-done((s32[1,16,16,16]{3,2,1,0:T(8,128)S(1)}, s32[1,16,16,16]{3,2,1,0:T(8,128)}, u32[]{:S(2)}) %copy-start.3) | copy-done | bytes 16408
  5.1 0.0 copy-start.4
  5.1 0.9 %copy-done.4 = f32[1,16,16,16]{3,2,1,0:T(8,128)S(1)} copy-done((f32[1,16,16,16]{3,2,1,0:T(8,128)S(1)}, f32[1,16,16,16]{3,2,1,0:T(8,128)}, u32[]{:S(2)}) %copy-start.4) | copy-done | bytes 16408
  6.0 34.6 %mmode.1 = f32[16,16,128]{2,1,0:T(8,128)S(1)} custom-call(bf16[8,16,1024]{2,1,0:T(8,128)(2,1)S(1)} %copy-done.2, f32[16,2,512,1024]{3,2,1,0:T(8,128)} %vis.1, bf16[16,8,64,128]{3,2,1,0:T(8,128)(2,1)S(1)} %copy-done, s32[16,16,16]{2,1,0:T(8,128)S(1)} %bitcast.4, f32[16,16,16]{2,1,0:T(8,128)S(1)} %bitcast.5, f32[16,64,64]{2,1,0:T(8,128)S(1)} %copy-done.1, ...), custom_call_target="tpu_custom_call" | custom-call | tf_op jit(solution)/shard_map/mmode/pallas_call | solution.py:274
  40.6 0.7 %copy.10 = f32[1,16,16,128]{3,2,1,0:T(8,128)} copy(f32[1,16,16,128]{3,2,1,0:T(8,128)S(1)} %bitcast.3) | data formatting | bytes 262144
Async XLA Ops:
  0.7 1.6 %copy-start = (bf16[16,8,64,128]{3,2,1,0:T(8,128)(2,1)S(1)}, bf16[16,8,64,128]{3,2,1,0:T(8,128)(2,1)}, u32[]{:S(2)}) copy-start(bf16[16,8,64,128]{3,2,1,0:T(8,128)(2,1)} %cb_hbm.1) | copy-start | bytes 6291460
  2.2 1.0 %copy-start.1 = (f32[16,64,64]{2,1,0:T(8,128)S(1)}, f32[16,64,64]{2,1,0:T(8,128)}, u32[]{:S(2)}) copy-start(f32[16,64,64]{2,1,0:T(8,128)} %bas_hbm.1) | copy-start | bytes 786436
  3.3 0.9 %copy-start.2 = (bf16[8,16,1024]{2,1,0:T(8,128)(2,1)S(1)}, bf16[8,16,1024]{2,1,0:T(8,128)(2,1)}, u32[]{:S(2)}) copy-start(bf16[8,16,1024]{2,1,0:T(8,128)(2,1)} %constant.2.clone.tab_hbm) | copy-start | bytes 786436
  4.2 0.9 %copy-start.3 = (s32[1,16,16,16]{3,2,1,0:T(8,128)S(1)}, s32[1,16,16,16]{3,2,1,0:T(8,128)}, u32[]{:S(2)}) copy-start(s32[1,16,16,16]{3,2,1,0:T(8,128)} %param.9) | copy-start | bytes 49156
  5.1 0.9 %copy-start.4 = (f32[1,16,16,16]{3,2,1,0:T(8,128)S(1)}, f32[1,16,16,16]{3,2,1,0:T(8,128)}, u32[]{:S(2)}) copy-start(f32[1,16,16,16]{3,2,1,0:T(8,128)} %param.10) | copy-start | bytes 49156

commit v2 on v1

--- a/solution.py
+++ b/solution.py
@@ -12,6 +12,8 @@
 ELLS = 1024
 LANES = 256
 SUB = 8
+BATCH = 4
+DEPTH = 4
 MESH = pl.DeviceIdType.MESH
 NT = (((1,), (1,)), ((), ()))
 
@@ -26,24 +28,25 @@
     sine = np.sin(angle).reshape(modes_all, parts, time_dev).transpose(1, 0, 2)
     real_rows = np.concatenate([cosine, sine], axis=2)
     imag_rows = np.concatenate([-sine, cosine], axis=2)
-    return np.concatenate([real_rows, imag_rows], axis=1).astype(jnp.bfloat16)
+    return np.concatenate([real_rows, imag_rows], axis=1).astype(np.float32)
 
 
 def kernel(
     n_tm, n_fr, norm,
-    tab_hbm, vis, cb_hbm, idx_hbm, scl_hbm, bas_hbm, count,
+    tab_hbm, vis, cb_hbm, idx_hbm, scl_hbm, bas_hbm, cnt_hbm,
     out,
-    tab, cb, idx, scl, bas, vbuf, acc, send, recv, idx_t, scl_t, sel, vec, comb, filt, gath,
+    tab, cb, idx, scl, bas, tab_in, count, vbuf, acc, send, recv, idx_t, scl_t, sel, vec, comb, filt, gath,
     small_sem, vis_sem, send_sem, recv_sem, gsend_sem, grecv_sem,
 ):
     tm = lax.axis_index("tm")
     fr = lax.axis_index("freq")
     modes = tab.shape[0] // 2
-    samples = vbuf.shape[2]
+    samples = vbuf.shape[3]
     chans = vis.shape[0]
     halves = chans // SUB
     lane_groups = vis.shape[3] // LANES
     groups = lane_groups * halves
+    piece = min(256, samples)
     blocks = vec.shape[1]
     bands, codes = cb.shape[0], cb.shape[1]
     f32, bf16 = jnp.float32, jnp.bfloat16
@@ -51,21 +54,26 @@
     smalls = [
         pltpu.make_async_copy(src, dst, small_sem.at[i])
         for i, (src, dst) in enumerate(
-            ((idx_hbm, idx), (scl_hbm, scl), (tab_hbm.at[tm], tab), (bas_hbm, bas), (cb_hbm, cb))
+            (
+                (idx_hbm, idx), (scl_hbm, scl), (tab_hbm.at[tm], tab_in), (bas_hbm, bas), (cb_hbm, cb),
+                (cnt_hbm, count),
+            )
         )
     ]
 
-    def fetch(g, slot):
+    def fetch(step, slot):
+        per_group = SUB // BATCH
+        g = step // per_group
         lanes = pl.ds(pl.multiple_of((g // halves) * LANES, LANES), LANES)
-        chan = (g % halves) * SUB + slot
+        chan = (g % halves) * SUB + (step % per_group) * BATCH
         return pltpu.make_async_copy(
-            vis.at[chan, :, :, lanes], vbuf.at[slot], vis_sem.at[slot]
+            vis.at[pl.ds(chan, BATCH), :, :, lanes], vbuf.at[slot], vis_sem.at[slot]
         )
 
     for copy in smalls[:3]:
         copy.start()
-    for slot in range(SUB):
-        fetch(0, slot).start()
+    for slot in range(DEPTH):
+        fetch(slot, slot).start()
     for copy in smalls[3:]:
         copy.start()
 
@@ -108,6 +116,7 @@
             ).astype(bf16)
 
     smalls[2].wait()
+    tab[...] = tab_in[...].astype(bf16)
     pl.semaphore_wait(barrier, n_tm - 1 + n_fr - 1)
 
     def take(lane_group):
@@ -143,16 +152,24 @@
         @pl.loop(0, halves)
         def _(half):
             g = lane_group * halves + half
-            for slot in range(SUB):
-                fetch(g, slot).wait()
-                block = vbuf[slot].reshape(2 * samples, LANES).astype(bf16)
-                sums = jnp.dot(tab[...], block, preferred_element_type=f32)
-                acc[:, slot, :] = sums[:modes]
-                acc[:, SUB + slot, :] = sums[modes:]
-
-                @pl.when(g + 1 < groups)
+            for part in range(SUB // BATCH):
+                step = g * (SUB // BATCH) + part
+                slot = lax.rem(step, DEPTH)
+                fetch(step, slot).wait()
+                for i in range(BATCH):
+                    sums = jnp.zeros((2 * modes, LANES), f32)
+                    for c in range(2):
+                        for t in range(0, samples, piece):
+                            block = vbuf[slot, i, c, t : t + piece, :].astype(bf16)
+                            table = tab[:, c * samples + t : c * samples + t + piece]
+                            sums += jnp.dot(table, block, preferred_element_type=f32)
+                    chan = part * BATCH + i
+                    acc[:, chan, :] = sums[:modes]
+                    acc[:, SUB + chan, :] = sums[modes:]
+
+                @pl.when(step + DEPTH < groups * (SUB // BATCH))
                 def _():
-                    fetch(g + 1, slot).start()
+                    fetch(step + DEPTH, slot).start()
 
             send[g] = (acc[...] * f32(norm)).astype(bf16)
             pltpu.make_async_copy(send.at[g, tm], recv.at[g, tm], recv_sem.at[g]).start()
@@ -175,6 +192,7 @@
 
     smalls[3].wait()
     smalls[4].wait()
+    smalls[5].wait()
     part = bands // 2
     all_chans = bas.shape[1]
     rows = chans * part
@@ -234,9 +252,8 @@
         for d in range(1, n_fr):
             share(h, d).start()
 
-    kept = (
-        lax.broadcasted_iota(jnp.int32, (chans, part, 128), 0) + fr * chans >= count[0]
-    )
+    mode_index = lax.broadcasted_iota(jnp.int32, (chans, part, 128), 0) + fr * chans
+    kept = mode_index >= count[...].reshape(1, 1, 1)
     for h in range(2):
         for d in range(1, n_fr):
             share(h, d).wait_recv()
@@ -269,12 +286,12 @@
     wide = blocks * chans
     norm = float(time_dev * n_tm) ** -0.5
     tables = jnp.asarray(phase_tables(n_tm, time_dev, modes_all))
-    anywhere = pl.BlockSpec(memory_space=pl.ANY)
+    anywhere = pl.BlockSpec(memory_space=pltpu.HBM)
     f32, bf16 = jnp.float32, jnp.bfloat16
     out = pl.pallas_call(
         functools.partial(kernel, n_tm, n_fr, norm),
         out_shape=jax.ShapeDtypeStruct((chans, bands, width), f32),
-        in_specs=[anywhere] * 6 + [pl.BlockSpec(memory_space=pltpu.SMEM)],
+        in_specs=[anywhere] * 7,
         out_specs=pl.BlockSpec(memory_space=pltpu.VMEM),
         scratch_shapes=[
             pltpu.VMEM(tables.shape[1:], bf16),
@@ -282,7 +299,9 @@
             pltpu.VMEM(block_index.shape[1:], jnp.int32),
             pltpu.VMEM(block_scale.shape[1:], f32),
             pltpu.VMEM(fg_basis.shape, f32),
-            pltpu.VMEM((SUB, 2, time_dev, LANES), f32),
+            pltpu.VMEM(tables.shape[1:], f32),
+            pltpu.VMEM((1, 1), jnp.int32),
+            pltpu.VMEM((DEPTH, BATCH, 2, time_dev, LANES), f32),
             pltpu.VMEM((modes_all, 2 * SUB, LANES), f32),
             pltpu.VMEM((groups, n_tm, 2 * SUB, LANES), bf16),
             pltpu.VMEM((groups, n_tm, 2 * SUB, LANES), bf16),
@@ -293,15 +312,15 @@
             pltpu.VMEM((bands // 2, codes // 2 * chans, LANES), bf16),
             pltpu.VMEM((chans * (bands // 2), bands * all_chans), bf16),
             pltpu.VMEM((n_fr, bands, chans, width), bf16),
-            pltpu.SemaphoreType.DMA((5,)),
-            pltpu.SemaphoreType.DMA((SUB,)),
+            pltpu.SemaphoreType.DMA((6,)),
+            pltpu.SemaphoreType.DMA((DEPTH,)),
             pltpu.SemaphoreType.DMA((groups,)),
             pltpu.SemaphoreType.DMA((groups,)),
             pltpu.SemaphoreType.DMA((2, n_fr - 1)),
             pltpu.SemaphoreType.DMA((2, n_fr - 1)),
         ],
         compiler_params=pltpu.CompilerParams(
-            collective_id=0, has_side_effects=True, vmem_limit_bytes=48 * 1024 * 1024
+            collective_id=0, has_side_effects=True, vmem_limit_bytes=62 * 1024 * 1024
         ),
         name="mmode",
     )(
@@ -311,7 +330,7 @@
         block_index.reshape(block_index.shape[1:]),
         block_scale.reshape(block_scale.shape[1:]),
         fg_basis,
-        fg_count,
+        fg_count.reshape(1, 1),
     )
     return out[None]
 

time: 41.5 us -> 38.1 us (0.918)
  local copies, waits for them, and re-layouts: 6.04 us -> 1.57 us
  Pallas kernels: 34.6 us -> 35.7 us
    unnamed x11 -> x1, local copies, waits for them, and re-layouts: 6.04 us -> 1.57 us
    pallas_call x1, Pallas kernels: 34.6 us -> 35.7 us  [local(): pl.pallas_call(functools.partial(kernel, n_tm, n_fr, norm), out_shape=jax...]
where the time goes in v2:
time: 38.1 us; the launch traced here: 37.9 us
  Pallas kernels  35.7 us (94%)
  local copies, waits for them, and re-layouts  1.57 us (4%)
  between operations  0.66 us (2%)
    pallas_call x1, Pallas kernels, local(): pl.pallas_call(functools.partial(kernel, n_tm, n_fr, norm), out_shape=jax...  35.7 us
    unnamed x1, local copies, waits for them, and re-layouts  1.57 us

profile of v2, /device:TPU:0, one launch (start us, length us, event | category | flops | bytes accessed | tf_op | source)
XLA Modules:
  0.0 37.9 jit_solution(6949338398028276626)
XLA Ops:
  0.7 35.7 %mmode.1 = f32[16,16,128]{2,1,0:T(8,128)} custom-call(f32[8,16,1024]{2,1,0:T(8,128)} %constant.2.clone.tab_hbm, f32[16,2,512,1024]{3,2,1,0:T(8,128)} %vis.1, bf16[16,8,64,128]{3,2,1,0:T(8,128)(2,1)} %cb_hbm.1, s32[16,16,16]{2,1,0:T(8,128)} %bitcast.6, f32[16,16,16]{2,1,0:T(8,128)} %bitcast.7, f32[16,64,64]{2,1,0:T(8,128)} %bas_hbm.1, s32[1,1]{1,0:T(1,128)} %bitcast.4.cnt_hbm), custom_call_target="tpu_custom_call" | custom-call | tf_op jit(solution)/shard_map/mmode/pallas_call | solution.py:291
  36.3 1.6 %copy.10 = f32[1,16,16,128]{3,2,1,0:T(8,128)} copy(f32[1,16,16,128]{3,2,1,0:T(8,128)} %bitcast.5) | data formatting | bytes 262144

commit v3 on v2

--- a/solution.py
+++ b/solution.py
@@ -10,9 +10,10 @@
 from jax.sharding import PartitionSpec as P
 
 ELLS = 1024
-LANES = 256
+LANES = 512
+QUAD = 256
 SUB = 8
-BATCH = 4
+BATCH = 2
 DEPTH = 4
 MESH = pl.DeviceIdType.MESH
 NT = (((1,), (1,)), ((), ()))
@@ -210,7 +211,7 @@
 
     take(lane_groups - 1)
 
-    vectors = vec[...].reshape(2 * wide, LANES)
+    vectors = vec[...].reshape(2 * wide, QUAD)
     left = lax.broadcasted_iota(jnp.int32, (chans, 128), 1) < 64
     pairs = codes // 2
 
@@ -231,7 +232,7 @@
         comb[...] = (
             jnp.dot(chosen, vectors, preferred_element_type=f32)
             .astype(bf16)
-            .reshape(part, pairs * chans, LANES)
+            .reshape(part, pairs * chans, QUAD)
         )
         for k in range(part):
             c = comb[k]
@@ -308,8 +309,8 @@
             pltpu.VMEM((bands, wide), f32),
             pltpu.VMEM((bands, wide), f32),
             pltpu.VMEM((bands, codes // 2 * chans, 2 * wide), bf16),
-            pltpu.VMEM((2, blocks, chans, LANES), bf16),
-            pltpu.VMEM((bands // 2, codes // 2 * chans, LANES), bf16),
+            pltpu.VMEM((2, blocks, chans, QUAD), bf16),
+            pltpu.VMEM((bands // 2, codes // 2 * chans, QUAD), bf16),
             pltpu.VMEM((chans * (bands // 2), bands * all_chans), bf16),
             pltpu.VMEM((n_fr, bands, chans, width), bf16),
             pltpu.SemaphoreType.DMA((6,)),

time: 38.1 us -> 38 us (level)
  no operation moved by 1% of the time
where the time goes in v3:
time: 38 us; the launch traced here: 37.8 us
  Pallas kernels  35.6 us (94%)
  local copies, waits for them, and re-layouts  1.57 us (4%)
  between operations  0.66 us (2%)
    pallas_call x1, Pallas kernels, local(): pl.pallas_call(functools.partial(kernel, n_tm, n_fr, norm), out_shape=jax...  35.6 us
    unnamed x1, local copies, waits for them, and re-layouts  1.57 us

profile of v3, /device:TPU:0, one launch (start us, length us, event | category | flops | bytes accessed | tf_op | source)
XLA Modules:
  0.0 37.8 jit_solution(11080154820826117129)
XLA Ops:
  0.7 35.6 %mmode.1 = f32[16,16,128]{2,1,0:T(8,128)} custom-call(f32[8,16,1024]{2,1,0:T(8,128)} %constant.2.clone.tab_hbm, f32[16,2,512,1024]{3,2,1,0:T(8,128)} %vis.1, bf16[16,8,64,128]{3,2,1,0:T(8,128)(2,1)} %cb_hbm.1, s32[16,16,16]{2,1,0:T(8,128)} %bitcast.6, f32[16,16,16]{2,1,0:T(8,128)} %bitcast.7, f32[16,64,64]{2,1,0:T(8,128)} %bas_hbm.1, s32[1,1]{1,0:T(1,128)} %bitcast.4.cnt_hbm), custom_call_target="tpu_custom_call" | custom-call | tf_op jit(solution)/shard_map/mmode/pallas_call | solution.py:292
  36.3 1.6 %copy.10 = f32[1,16,16,128]{3,2,1,0:T(8,128)} copy(f32[1,16,16,128]{3,2,1,0:T(8,128)} %bitcast.5) | data formatting | bytes 262144

commit v4 on v2

--- a/solution.py
+++ b/solution.py
@@ -320,7 +320,7 @@
             pltpu.SemaphoreType.DMA((2, n_fr - 1)),
         ],
         compiler_params=pltpu.CompilerParams(
-            collective_id=0, has_side_effects=True, vmem_limit_bytes=62 * 1024 * 1024
+            collective_id=0, has_side_effects=True, vmem_limit_bytes=55040 * 1024
         ),
         name="mmode",
     )(

time: 38.1 us -> 36.5 us (0.958)
  local copies, waits for them, and re-layouts: 1.57 us -> 0.66 us
  Pallas kernels: 35.7 us -> 35 us
    unnamed x1, local copies, waits for them, and re-layouts: 1.57 us -> 0.66 us
    pallas_call x1, Pallas kernels: 35.7 us -> 35 us  [local(): pl.pallas_call(functools.partial(kernel, n_tm, n_fr, norm), out_shape=jax...]
where the time goes in v4:
time: 36.5 us; the launch traced here: 36.4 us
  Pallas kernels  35 us (96%)
  local copies, waits for them, and re-layouts  0.66 us (2%)
  between operations  0.66 us (2%)
    pallas_call x1, Pallas kernels, local(): pl.pallas_call(functools.partial(kernel, n_tm, n_fr, norm), out_shape=jax...  35 us

profile of v4, /device:TPU:0, one launch (start us, length us, event | category | flops | bytes accessed | tf_op | source)
XLA Modules:
  0.0 36.4 jit_solution(17225025731201803397)
XLA Ops:
  0.7 35.0 %mmode.1 = f32[16,16,128]{2,1,0:T(8,128)S(1)} custom-call(f32[8,16,1024]{2,1,0:T(8,128)} %constant.2.clone.tab_hbm, f32[16,2,512,1024]{3,2,1,0:T(8,128)} %vis.1, bf16[16,8,64,128]{3,2,1,0:T(8,128)(2,1)} %cb_hbm.1, s32[16,16,16]{2,1,0:T(8,128)} %bitcast.6, f32[16,16,16]{2,1,0:T(8,128)} %bitcast.7, f32[16,64,64]{2,1,0:T(8,128)} %bas_hbm.1, s32[1,1]{1,0:T(1,128)} %bitcast.4.cnt_hbm), custom_call_target="tpu_custom_call" | custom-call | tf_op jit(solution)/shard_map/mmode/pallas_call | solution.py:291
  35.7 0.7 %copy.10 = f32[1,16,16,128]{3,2,1,0:T(8,128)} copy(f32[1,16,16,128]{3,2,1,0:T(8,128)S(1)} %bitcast.5) | data formatting | bytes 262144
